TPU v7x, 512 devices: a whole 4x4x16 slice. The times are simulated.
512 devices in a mesh: ov: 64 (over z, y_hi, core), vec: 8 (over x, y_lo).
Axes of the slice: x: 4, y: 4 (y_hi: 2, y_lo: 2; y = y_hi * 2 + y_lo), z: 16, core: 2. Of those that a mesh axis runs over, the one named last changes fastest.
Arguments:
- chol_vectors: bfloat16 [196608, 4096], P('ov', 'vec'), may hold values from -6 to 6
- amplitudes: bfloat16 [196608, 256], P('ov'), may hold values from -0.013671875 to 0.013671875
- sigma_prior: bfloat16 [196608, 256], P(('ov', 'vec')), may hold values from -4 to 4
Outputs:
- sigma_cycle: bfloat16 [196608, 256], P(('ov', 'vec'))
All inputs are finite; a program needn't handle non-finite values.
Results may differ from a plain program's by a relative error of at most 0.0065.
Values may be sent and summed in bfloat16 or wider, within the bound.
No kernel may reach another device: no remote copies, remote signals or barrier semaphores. Data moves between devices by JAX's collectives and lax.ppermute only.
A program may use at most 64 MiB of HBM per device.

v0:
```python
import jax
import jax.numpy as jnp
from jax import lax
from jax.sharding import Mesh
from jax.sharding import PartitionSpec as P

OV = ("ov_0", "ov_1", "ov_2")
OV_VEC = ("ov_0", "ov_1", "ov_2", "vec")


def rows_for(lines, count):
    spare = -len(lines) % count
    return jnp.pad(lines, [(0, spare)] + [(0, 0)] * (lines.ndim - 1))


def copy_for_each(x, axis):
    copies = jnp.broadcast_to(x, (lax.axis_size(axis), *x.shape))
    return lax.all_to_all(copies, axis, split_axis=0, concat_axis=0, tiled=True)


def joined_along(blocks, dim):
    blocks = jnp.moveaxis(blocks, 0, dim)
    lengths = blocks.shape
    return blocks.reshape(*lengths[:dim], lengths[dim] * lengths[dim + 1], *lengths[dim + 2 :])


def whole_of(x, axes, dim):
    far, near = axes
    blocks = copy_for_each(copy_for_each(x, far), near)
    return joined_along(blocks.swapaxes(0, 1).reshape(-1, *x.shape), dim)


def cut_along(x, dim, count):
    before, after = (x.shape[:dim], x.shape[dim + 1 :])
    return jnp.moveaxis(x.reshape(*before, count, -1, *after), dim, 0)


def sent_and_summed(x, axis, dim):
    blocks = cut_along(x, dim, lax.axis_size(axis))
    arrived = lax.all_to_all(blocks, axis, split_axis=0, concat_axis=0, tiled=True)
    return arrived.sum(axis=0)


def sum_by_axis(x, axes, dim):
    far, near = axes
    own = sent_and_summed(cut_along(x, dim, lax.axis_size(far)), near, dim + 1)
    return jnp.sum(lax.all_to_all(own, far, 0, 0, tiled=True), axis=0)


def sum_by_parts(x, axes):
    lines = x.reshape(-1, x.shape[-1])
    padded = rows_for(lines, lax.axis_size(axes[0]) * lax.axis_size(axes[1]))
    whole = whole_of(sum_by_axis(padded, axes, 0), axes, 0)
    return lax.slice_in_dim(whole, 0, len(lines)).reshape(x.shape)


def sum_at_owner(x, axis, dim):
    blocks = cut_along(x, dim, lax.axis_size(axis))
    arrived = lax.all_to_all(blocks, axis, split_axis=0, concat_axis=0, tiled=True)
    return arrived.astype(jnp.float32).sum(axis=0)


def body(chol_vectors, amplitudes, sigma_prior):
    contract = (((0,), (0,)), ((), ()))
    partial_x = lax.dot_general(
        chol_vectors, amplitudes, contract, preferred_element_type=jnp.float32
    )
    summed = sum_by_parts(partial_x, (("ov_0", "ov_1"), "ov_2"))
    coupling = summed.astype(jnp.bfloat16)
    cycle = sum_at_owner(
        jnp.dot(chol_vectors, coupling, preferred_element_type=jnp.float32).astype(jnp.bfloat16),
        "vec",
        0,
    )
    return (sigma_prior.astype(jnp.float32) + cycle).astype(jnp.bfloat16)


def solution(mesh):
    finer = Mesh(mesh.devices.reshape(16, 2, 2, mesh.shape["vec"]), ("ov_0", "ov_1", "ov_2", "vec"))
    placed = (P(OV, "vec"), P(OV, None), P(OV_VEC, None))
    return jax.shard_map(
        body, mesh=finer, in_specs=placed, out_specs=P(OV_VEC, None), check_vma=False
    )
```

profile of v0, /device:TPU:1, one launch (start us, length us, event | category | flops | bytes accessed | tf_op | source)
XLA Modules:
  0.0 110.5 jit_solution(3194452911068703950)
XLA Ops:
  0.0 0.0 copy-start
  0.0 1.9 %copy-done = bf16[3072,512]{1,0:T(8,128)(2,1)S(1)} copy-done((bf16[3072,512]{1,0:T(8,128)(2,1)S(1)}, bf16[3072,512]{1,0:T(8,128)(2,1)}, u32[]{:S(2)}) %copy-start) | copy-done | bytes 3145752
  1.9 2.4 %fusion = f32[512,256]{1,0:T(8,128)S(1)} fusion(bf16[3072,512]{1,0:T(8,128)(2,1)S(1)} %copy-done, bf16[3072,256]{1,0:T(8,128)(2,1)} %param.4), kind=kOutput, calls=%fused_computation.6 | convolution fusion | flops 805306368 | bytes 5242880 | tf_op jit(solution)/shard_map/dot_general | solution.py:65
  4.4 11.4 %all_to_all.25 = f32[2,32,8,256]{3,2,1,0:T(8,128)} all-to-all(f32[2,32,8,256]{3,2,1,0:T(8,128)S(1)} %bitcast.19), channel_id=1, replica_groups=mesh['ov_0'=16,'ov_1'=2,'ov_2'=2,'vec'=8] {'ov_2'}, dimensions={0} | all-to-all | bytes 1048576 | tf_op jit(solution)/shard_map/all_to_all | solution.py:40
  15.8 1.8 %reduce_sum.27 = f32[32,8,256]{2,1,0:T(8,128)} reduce(f32[2,32,8,256]{3,2,1,0:T(8,128)} %all_to_all.25, f32[]{:T(128)} %constant.1.clone.1), dimensions={0}, to_apply=%region_0.1 | reduce | flops 65536 | bytes 786436 | tf_op jit(solution)/shard_map/reduce_sum | solution.py:41
  17.6 33.4 %all_to_all.26 = f32[32,8,256]{2,1,0:T(8,128)S(1)} all-to-all(f32[32,8,256]{2,1,0:T(8,128)} %reduce_sum.27), channel_id=1, replica_groups=mesh['ov_0'=16,'ov_1'=2,'ov_2'=2,'vec'=8] {'ov_0','ov_1'}, dimensions={0} | all-to-all | bytes 524288 | tf_op jit(solution)/shard_map/all_to_all | solution.py:47
  51.0 19.7 %all_to_all.27 = bf16[32,8,256]{2,1,0:T(8,128)(2,1)S(1)} all-to-all(bf16[32,8,256]{2,1,0:T(8,128)(2,1)S(1)} %broadcast_in_dim.6), channel_id=1, replica_groups=mesh['ov_0'=16,'ov_1'=2,'ov_2'=2,'vec'=8] {'ov_0','ov_1'}, dimensions={0} | all-to-all | bytes 262144 | tf_op jit(solution)/shard_map/all_to_all | solution.py:18
  70.7 6.9 %all_to_all.28 = bf16[2,32,8,256]{3,2,1,0:T(8,128)(2,1)S(1)} all-to-all(bf16[2,32,8,256]{3,2,1,0:T(8,128)(2,1)S(1)} %broadcast_in_dim.7), channel_id=1, replica_groups=mesh['ov_0'=16,'ov_1'=2,'ov_2'=2,'vec'=8] {'ov_2'}, dimensions={0} | all-to-all | bytes 524288 | tf_op jit(solution)/shard_map/all_to_all | solution.py:18
  77.6 1.0 convolution_convert_fusion
  78.7 0.0 copy-start.1
  78.7 1.3 %copy.22 = bf16[32,8,8,384]{3,2,0,1:T(8,128)(2,1)} copy(bf16[32,8,8,384]{3,2,1,0:T(8,128)(2,1)S(1)} %bitcast.17) | data formatting | bytes 3145728 | tf_op jit(solution)/shard_map/reshape | solution.py:35
  80.0 4.5 %all-to-all-start.4 = ((bf16[8,384,256]{1,2,0:T(8,128)(2,1)}), bf16[8,384,256]{1,2,0:T(8,128)(2,1)}, u32[]{:S(2)}, u32[]{:S(2)}) async-start(bf16[8,384,256]{1,2,0:T(8,128)(2,1)} %bitcast.16), calls=%async_computation.4 | async-start | bytes 3145728 | tf_op jit(solution)/shard_map/all_to_all | solution.py:59
  84.5 0.0 copy-done.1
  84.5 0.2 copy.10
  84.7 23.3 %all-to-all-done.4 = bf16[8,384,256]{1,2,0:T(8,128)(2,1)} async-done(((bf16[8,384,256]{1,2,0:T(8,128)(2,1)}), bf16[8,384,256]{1,2,0:T(8,128)(2,1)}, u32[]{:S(2)}, u32[]{:S(2)}) %all-to-all-start.4) | async-done | bytes 1572896 | tf_op jit(solution)/shard_map/all_to_all | solution.py:59
  108.0 1.7 %convert_reduce_fusion = f32[384,256]{0,1:T(8,128)S(1)} fusion(bf16[8,384,256]{1,2,0:T(8,128)(2,1)} %all-to-all-done.4), kind=kLoop, calls=%fused_computation.1 | loop fusion | flops 1474560 | bytes 1966080 | tf_op jit(solution)/shard_map/reduce_sum | solution.py:60
  109.7 0.1 add_convert_fusion
  109.7 0.8 copy.15
  (5 shorter events, 0.1 us)
Async XLA Ops:
  0.0 1.9 %copy-start = (bf16[3072,512]{1,0:T(8,128)(2,1)S(1)}, bf16[3072,512]{1,0:T(8,128)(2,1)}, u32[]{:S(2)}) copy-start(bf16[3072,512]{1,0:T(8,128)(2,1)} %param.3) | copy-start | bytes 9437188
  78.7 5.8 %copy-start.1 = (bf16[384,256]{1,0:T(8,128)(2,1)S(1)}, bf16[384,256]{1,0:T(8,128)(2,1)}, u32[]{:S(2)}) copy-start(bf16[384,256]{1,0:T(8,128)(2,1)} %param.5) | copy-start | bytes 589828
  80.0 28.0 %all-to-all-start.4 = ((bf16[8,384,256]{1,2,0:T(8,128)(2,1)}), bf16[8,384,256]{1,2,0:T(8,128)(2,1)}, u32[]{:S(2)}, u32[]{:S(2)}) async-start(bf16[8,384,256]{1,2,0:T(8,128)(2,1)} %bitcast.16), calls=%async_computation.4 | async-start | bytes 3145728 | tf_op jit(solution)/shard_map/all_to_all | solution.py:59
where the time goes:
time: 111 us
  blocking collectives  71.4 us (64%)
  waiting for transfers between devices  23.3 us (21%)
  starting transfers between devices  4.49 us (4%)
  local copies, waits for them, and re-layouts  4.28 us (4%)
  other arithmetic  3.55 us (3%)
  matrix products  3.45 us (3%)
    all_to_all x1, blocking collectives, sum_by_axis(): return jnp.sum(lax.all_to_all(own, far, 0, 0, tiled=True), axis=0)  33.4 us
    all_to_all x2, blocking collectives, copy_for_each(): return lax.all_to_all(copies, axis, split_axis=0, concat_axis=0, tiled=True)  26.6 us
    all_to_all x1, waiting for transfers between devices, sum_at_owner(): lax.all_to_all(blocks, axis, split_axis=0, concat_axis=0, tiled=True)  23.3 us
    all_to_all x1, blocking collectives, sent_and_summed(): lax.all_to_all(blocks, axis, split_axis=0, concat_axis=0, tiled=True)  11.4 us
    all_to_all x1, starting transfers between devices, sum_at_owner(): lax.all_to_all(blocks, axis, split_axis=0, concat_axis=0, tiled=True)  4.49 us
    dot_general x1, matrix products, body(): lax.dot_general(chol_vectors, amplitudes, contract, preferred_element_typ...  2.42 us
  transfers between devices with their start and end apart: 1, of which 1 were waited for; matrix products, arithmetic and copies ran while one was open for 0% of the time, Pallas kernels for 0%

commit v1 on v0

v1 whole, which is shorter than its diff:
```python
import jax
import jax.numpy as jnp
from jax import lax
from jax.experimental import pallas as pl
from jax.experimental.pallas import tpu as pltpu
from jax.sharding import Mesh
from jax.sharding import PartitionSpec as P

FAR, NEAR, YH, CORE, VEC = "z_far", "z_near", "y_hi", "core", "vec"
OV = (FAR, NEAR, YH, CORE)
BLOCK = (NEAR, YH)


def exchange(blocks, axes):
    return lax.all_to_all(blocks, axes, split_axis=0, concat_axis=0, tiled=True)


def sum_of_blocks(blocks):
    return blocks.astype(jnp.float32).sum(axis=0).astype(jnp.bfloat16)


def scatter_sum(x, axes):
    return sum_of_blocks(exchange(x.reshape(lax.axis_size(axes), -1, x.shape[-1]), axes))


def copies(x, axes):
    return exchange(jnp.broadcast_to(x, (lax.axis_size(axes), *x.shape)), axes)


def gather(x, axes):
    return copies(x, axes).reshape(-1, x.shape[-1])


def product_kernel(l_ref, c_ref, out_ref):
    out_ref[...] = jnp.dot(
        l_ref[...], c_ref[...], preferred_element_type=jnp.float32
    ).astype(jnp.bfloat16)


def product(chol, coupling):
    rows, depth = chol.shape
    cols = coupling.shape[1]
    tile = rows // 4
    return pl.pallas_call(
        product_kernel,
        grid=(4,),
        in_specs=[
            pl.BlockSpec((tile, depth), lambda i: (i, 0)),
            pl.BlockSpec((depth, cols), lambda i: (0, 0)),
        ],
        out_specs=pl.BlockSpec((tile, cols), lambda i: (i, 0)),
        out_shape=jax.ShapeDtypeStruct((rows, cols), jnp.bfloat16),
        cost_estimate=pl.CostEstimate(
            flops=2 * rows * depth * cols,
            bytes_accessed=2 * (rows * depth + depth * cols + rows * cols),
            transcendentals=0,
        ),
    )(chol, coupling)


def body(chol_vectors, amplitudes, sigma_prior):
    contract = (((0,), (0,)), ((), ()))
    partial = lax.dot_general(
        chol_vectors, amplitudes, contract, preferred_element_type=jnp.float32
    ).astype(jnp.bfloat16)
    piece = scatter_sum(scatter_sum(partial, CORE), BLOCK)
    piece = sum_of_blocks(copies(piece, FAR))
    coupling = gather(gather(piece, BLOCK), CORE)
    share = product(chol_vectors, coupling)
    arrived = exchange(share.reshape(lax.axis_size(VEC), -1, share.shape[-1]), VEC)
    cycle = arrived.astype(jnp.float32).sum(axis=0)
    return (sigma_prior.astype(jnp.float32) + cycle).astype(jnp.bfloat16)


def solution(mesh):
    finer = Mesh(mesh.devices.reshape(4, 4, 2, 2, mesh.shape["vec"]), (*OV, VEC))
    placed = (P(OV, VEC), P(OV, None), P((*OV, VEC), None))
    return jax.shard_map(
        body, mesh=finer, in_specs=placed, out_specs=P((*OV, VEC), None), check_vma=False
    )
```

time: 111 us -> 99.1 us (0.89)
  waiting for transfers between devices: 23.3 us -> 0 us
  blocking collectives: 71.4 us -> 87.7 us
  Pallas kernels: 0 us -> 4.62 us
  starting transfers between devices: 4.49 us -> 0 us
  other arithmetic: 3.55 us -> 1.02 us
  local copies, waits for them, and re-layouts: 4.28 us -> 2.15 us
    all_to_all x1 -> x0, waiting for transfers between devices: 23.3 us -> none  [sum_at_owner(): lax.all_to_all(blocks, axis, split_axis=0, concat_axis=0, tiled=True)]
    all_to_all x4 -> x6, blocking collectives: 71.4 us -> 87.7 us  [exchange(): return lax.all_to_all(blocks, axes, split_axis=0, concat_axis=0, tiled=True)]
    pallas_call x0 -> x1, Pallas kernels: none -> 4.62 us  [product(): pl.pallas_call(product_kernel, grid=(4,), in_specs=[pl.BlockSpec((tile, d...]
    all_to_all x1 -> x0, starting transfers between devices: 4.49 us -> none  [sum_at_owner(): lax.all_to_all(blocks, axis, split_axis=0, concat_axis=0, tiled=True)]
    reduce_sum x3 -> x4, other arithmetic: 3.5 us -> 0.3 us  [the longest x1 0.22 us: body(): cycle = arrived.astype(jnp.float32).sum(axis=0)]
    reshape x1 -> x0, local copies, waits for them, and re-layouts: 1.32 us -> none  [cut_along(): return jnp.moveaxis(x.reshape(*before, count, -1, *after), dim, 0)]
  transfers between devices with their start and end apart: 1 -> 0, of which waited for: 1 -> 0; matrix products, arithmetic and copies ran while one was open for 0% -> 0% of each run, Pallas kernels for 0% -> 0%
where the time goes in v1:
time: 99.1 us; the launch traced here: 98.4 us
  blocking collectives  87.7 us (88%)
  Pallas kernels  4.62 us (5%)
  matrix products  2.91 us (3%)
  local copies, waits for them, and re-layouts  2.15 us (2%)
  other arithmetic  1.02 us (1%)
    all_to_all x6, blocking collectives, exchange(): return lax.all_to_all(blocks, axes, split_axis=0, concat_axis=0, tiled=True)  87.7 us
    pallas_call x1, Pallas kernels, product(): pl.pallas_call(product_kernel, grid=(4,), in_specs=[pl.BlockSpec((tile, d...  4.62 us
    dot_general x1, matrix products, body(): lax.dot_general(chol_vectors, amplitudes, contract, preferred_element_typ...  2.91 us
    unnamed x4, local copies, waits for them, and re-layouts  2.12 us

profile of v1, /device:TPU:1, one launch (start us, length us, event | category | flops | bytes accessed | tf_op | source)
XLA Modules:
  0.0 98.4 jit_solution(2811857012800107762)
XLA Ops:
  0.0 0.0 copy-start
  0.0 1.4 %copy-done = bf16[3072,256]{1,0:T(8,128)(2,1)S(1)} copy-done((bf16[3072,256]{1,0:T(8,128)(2,1)S(1)}, bf16[3072,256]{1,0:T(8,128)(2,1)}, u32[]{:S(2)}) %copy-start) | copy-done | bytes 1572888
  1.4 2.9 %convolution_convert_fusion = bf16[512,256]{1,0:T(8,128)(2,1)S(1)} fusion(bf16[3072,512]{1,0:T(8,128)(2,1)} %l_ref.1, bf16[3072,256]{1,0:T(8,128)(2,1)S(1)} %copy-done), kind=kOutput, calls=%fused_computation.1 | convolution fusion | flops 805437440 | bytes 4980736 | tf_op jit(solution)/shard_map/dot_general | solution.py:63
  4.3 10.5 %all_to_all.30 = bf16[2,256,256]{2,1,0:T(8,128)(2,1)S(1)} all-to-all(bf16[2,256,256]{2,1,0:T(8,128)(2,1)S(1)} %bitcast.9), channel_id=1, replica_groups=mesh['z_far'=4,'z_near'=4,'y_hi'=2,'core'=2,'vec'=8] {'core'}, dimensions={0} | all-to-all | bytes 524288 | tf_op jit(solution)/shard_map/all_to_all | solution.py:15
  14.8 10.4 %all_to_all.31 = bf16[8,32,256]{2,1,0:T(8,128)(2,1)S(1)} all-to-all(bf16[8,32,256]{2,1,0:T(8,128)(2,1)S(1)} %bitcast.11), channel_id=1, replica_groups=mesh['z_far'=4,'z_near'=4,'y_hi'=2,'core'=2,'vec'=8] {'z_near','y_hi'}, dimensions={0} | all-to-all | bytes 262144 | tf_op jit(solution)/shard_map/all_to_all | solution.py:15
  25.3 24.1 %all_to_all.32 = bf16[4,32,256]{2,1,0:T(8,128)(2,1)S(1)} all-to-all(bf16[4,32,256]{2,1,0:T(8,128)(2,1)S(1)} %broadcast_in_dim.9), channel_id=1, replica_groups=mesh['z_far'=4,'z_near'=4,'y_hi'=2,'core'=2,'vec'=8] {'z_far'}, dimensions={0} | all-to-all | bytes 131072 | tf_op jit(solution)/shard_map/all_to_all | solution.py:15
  49.4 10.5 %all_to_all.33 = bf16[8,32,256]{2,1,0:T(8,128)(2,1)S(1)} all-to-all(bf16[8,32,256]{2,1,0:T(8,128)(2,1)S(1)} %broadcast_in_dim.10), channel_id=1, replica_groups=mesh['z_far'=4,'z_near'=4,'y_hi'=2,'core'=2,'vec'=8] {'z_near','y_hi'}, dimensions={0} | all-to-all | bytes 262144 | tf_op jit(solution)/shard_map/all_to_all | solution.py:15
  60.0 8.2 %all_to_all.34 = bf16[2,256,256]{2,1,0:T(8,128)(2,1)} all-to-all(bf16[2,256,256]{2,1,0:T(8,128)(2,1)S(1)} %broadcast_in_dim.11), channel_id=1, replica_groups=mesh['z_far'=4,'z_near'=4,'y_hi'=2,'core'=2,'vec'=8] {'core'}, dimensions={0} | all-to-all | bytes 524288 | tf_op jit(solution)/shard_map/all_to_all | solution.py:15
  68.2 4.6 %shard_map.37 = bf16[3072,256]{1,0:T(8,128)(2,1)} custom-call(bf16[3072,512]{1,0:T(8,128)(2,1)} %l_ref.1, bf16[512,256]{1,0:T(8,128)(2,1)} %bitcast.8), custom_call_target="tpu_custom_call" | custom-call | flops 805306368 | bytes 4980736 | tf_op jit(solution)/shard_map/pallas_call | solution.py:44
  72.8 24.0 %all_to_all.35 = bf16[8,384,256]{2,1,0:T(8,128)(2,1)S(1)} all-to-all(bf16[8,384,256]{2,1,0:T(8,128)(2,1)} %bitcast.7), channel_id=1, replica_groups=mesh['z_far'=4,'z_near'=4,'y_hi'=2,'core'=2,'vec'=8] {'vec'}, dimensions={0} | all-to-all | bytes 3145728 | tf_op jit(solution)/shard_map/all_to_all | solution.py:15
  96.8 0.0 copy-start.1
  96.8 0.2 convert_reduce_fusion
  97.0 0.7 copy-done.1
  97.7 0.7 add_convert_fusion
  (6 shorter events, 0.1 us)
Async XLA Ops:
  0.0 1.4 %copy-start = (bf16[3072,256]{1,0:T(8,128)(2,1)S(1)}, bf16[3072,256]{1,0:T(8,128)(2,1)}, u32[]{:S(2)}) copy-start(bf16[3072,256]{1,0:T(8,128)(2,1)} %param.4) | copy-start | bytes 4718596
  96.8 0.9 copy-start.1

commit v2 on v1

v2 whole, which is shorter than its diff:
```python
import jax
import jax.numpy as jnp
from jax import lax
from jax.experimental import pallas as pl
from jax.experimental.pallas import tpu as pltpu
from jax.sharding import Mesh
from jax.sharding import PartitionSpec as P

FAR, NEAR, YH, CORE, X, YL = "z_far", "z_near", "y_hi", "core", "x", "y_lo"
SIZES = (4, 4, 2, 2, 4, 2)
OV, VEC = (FAR, NEAR, YH, CORE), (X, YL)
SWAP = [(0, 1), (1, 0)]
LIMIT = 24 << 20
WHOLE = pl.BlockSpec(memory_space=pltpu.VMEM)
IN_HBM = pl.BlockSpec(memory_space=pltpu.HBM)
ROWS_BY_ROWS = (((0,), (0,)), ((), ()))
COLUMNS_BY_COLUMNS = (((1,), (1,)), ((), ()))


def in_hbm(x):
    return pltpu.with_memory_space_constraint(x, pltpu.HBM)


def in_vmem(x):
    return pltpu.with_memory_space_constraint(x, pltpu.VMEM)


def exchange(blocks, axes):
    return lax.all_to_all(blocks, axes, split_axis=0, concat_axis=0, tiled=True)


def copies(x, axes):
    return exchange(jnp.broadcast_to(x, (lax.axis_size(axes), *x.shape)), axes)


def summed(blocks):
    return blocks.astype(jnp.float32).sum(axis=0).astype(jnp.bfloat16)


def coupling_kernel(l_hbm, a_hbm, part_ref, kept_ref, sent_hbm, l_ref, a_ref, total_ref, l_sems, a_sems, sent_sems):
    mine = lax.axis_index(YL)
    blocks = l_sems.shape[0] // 2
    size = kept_ref.shape[0] // blocks

    def source(slot, block):
        start = (2 * block + (mine + slot) % 2) * size
        return pl.ds(pl.multiple_of(start, size), size)

    def fetches(k):
        slot, block = 1 - k // blocks, k % blocks
        rows = pl.ds(block * size, size)
        held = l_ref if slot else kept_ref
        return (
            pltpu.make_async_copy(a_hbm.at[source(slot, block)], a_ref.at[slot, rows], a_sems.at[k]),
            pltpu.make_async_copy(l_hbm.at[source(slot, block)], held.at[rows], l_sems.at[k]),
        )

    def passing(block):
        rows = pl.ds(block * size, size)
        return pltpu.make_async_copy(l_ref.at[rows], sent_hbm.at[rows], sent_sems.at[block])

    for k in range(2 * blocks):
        for copy in fetches(k):
            copy.start()
    for k in range(0, 2 * blocks, 2):
        for copy in (*fetches(k), *fetches(k + 1)):
            copy.wait()
        slot, rows = 1 - k // blocks, pl.ds(k % blocks * size, 2 * size)
        if slot:
            passing(k).start()
            passing(k + 1).start()
        held = l_ref if slot else kept_ref
        term = lax.dot_general(
            a_ref[slot, rows], held[rows], ROWS_BY_ROWS, preferred_element_type=jnp.float32
        )
        if k == 0:
            total_ref[...] = term
        elif k < 2 * blocks - 2:
            total_ref[...] += term
        else:
            part_ref[...] = (total_ref[...] + term).astype(jnp.bfloat16)
    for block in range(blocks):
        passing(block).wait()


def coupling_part(chol, amplitudes):
    rows, depth = chol.shape
    cols = amplitudes.shape[1]
    blocks = lax.axis_size(X)
    half = jax.ShapeDtypeStruct((rows // 2, depth), jnp.bfloat16)
    return pl.pallas_call(
        coupling_kernel,
        in_specs=[IN_HBM] * 2,
        out_specs=[WHOLE, WHOLE, IN_HBM],
        out_shape=[jax.ShapeDtypeStruct((cols, depth), jnp.bfloat16), half, pltpu.HBM(half.shape, half.dtype)],
        scratch_shapes=[
            pltpu.VMEM(half.shape, half.dtype),
            pltpu.VMEM((2, rows // 2, cols), jnp.bfloat16),
            pltpu.VMEM((cols, depth), jnp.float32),
            pltpu.SemaphoreType.DMA((2 * blocks,)),
            pltpu.SemaphoreType.DMA((2 * blocks,)),
            pltpu.SemaphoreType.DMA((blocks,)),
        ],
        compiler_params=pltpu.CompilerParams(vmem_limit_bytes=LIMIT),
        cost_estimate=pl.CostEstimate(
            flops=2 * rows * depth * cols,
            bytes_accessed=2 * (2 * rows * depth + rows * cols + depth * cols),
            transcendentals=0,
        ),
    )(in_hbm(chol), in_hbm(amplitudes))


def product_kernel(kept_ref, came_ref, own_ref, other_ref, out_ref, c_ref):
    mine, core = lax.axis_index(YL), lax.axis_index(CORE)
    blocks, size, _ = out_ref.shape
    half = own_ref.shape[1]
    for at, ref in ((core, own_ref), (1 - core, other_ref)):
        c_ref[:, pl.ds(pl.multiple_of(at * half, half), half), :] = ref[...]
    own, other = c_ref[mine], c_ref[1 - mine]

    def by(x, coupling):
        return lax.dot_general(x, coupling, COLUMNS_BY_COLUMNS, preferred_element_type=jnp.float32)

    for k in range(blocks):
        rows = pl.ds(k * size, size)
        out_ref[k] = (by(kept_ref[rows], own) + by(came_ref[rows], other)).astype(jnp.bfloat16)


def product(kept, came, own, other):
    rows, depth = kept.shape
    cols = 2 * own.shape[1]
    blocks = lax.axis_size(X)
    return pl.pallas_call(
        product_kernel,
        in_specs=[WHOLE] * 4,
        out_specs=WHOLE,
        out_shape=jax.ShapeDtypeStruct((blocks, rows // blocks, cols), jnp.bfloat16),
        scratch_shapes=[pltpu.VMEM((2, cols, depth), jnp.bfloat16)],
        compiler_params=pltpu.CompilerParams(vmem_limit_bytes=LIMIT),
        cost_estimate=pl.CostEstimate(
            flops=4 * kept.size * cols,
            bytes_accessed=2 * (2 * kept.size + 2 * own.size + rows * cols),
            transcendentals=0,
        ),
    )(kept, in_vmem(came), own, other)


def finish_kernel(arrived_ref, prior_ref, out_ref):
    cycle = arrived_ref[0].astype(jnp.float32)
    for k in range(1, arrived_ref.shape[0]):
        cycle += arrived_ref[k].astype(jnp.float32)
    out_ref[...] = (prior_ref[...].astype(jnp.float32) + cycle).astype(jnp.bfloat16)


def finish(arrived, prior):
    return pl.pallas_call(
        finish_kernel,
        in_specs=[WHOLE, WHOLE],
        out_specs=WHOLE,
        out_shape=jax.ShapeDtypeStruct(prior.shape, jnp.bfloat16),
        compiler_params=pltpu.CompilerParams(vmem_limit_bytes=LIMIT),
        cost_estimate=pl.CostEstimate(
            flops=arrived.size, bytes_accessed=2 * (arrived.size + 2 * prior.size), transcendentals=0
        ),
    )(arrived, prior)


def body(chol_vectors, amplitudes, sigma_prior):
    part, kept, sent = coupling_part(chol_vectors, amplitudes)
    came = lax.ppermute(sent, YL, SWAP)
    near = (CORE, NEAR, YH)
    piece = summed(exchange(part.reshape(lax.axis_size(near), -1, part.shape[-1]), near))
    piece = summed(copies(piece, FAR))
    half = copies(piece, (YL, NEAR, YH))
    half = half.reshape(2, -1, half.shape[-1])
    share = product(kept, came, half, lax.ppermute(half, CORE, SWAP))
    return finish(exchange(share, X), sigma_prior)


def solution(mesh):
    finer = Mesh(mesh.devices.reshape(SIZES), (*OV, *VEC))
    placed = (P(OV, VEC), P(OV, None), P((*OV, *VEC), None))
    return jax.shard_map(
        body, mesh=finer, in_specs=placed, out_specs=P((*OV, *VEC), None), check_vma=False
    )
```

time: 99.1 us -> 84.6 us (0.85)
  blocking collectives: 87.7 us -> 50.5 us
  starting transfers between devices: 0 us -> 18 us
  waiting for transfers between devices: 0 us -> 9.67 us
  matrix products: 2.91 us -> 0 us
  local copies, waits for them, and re-layouts: 2.15 us -> 0.03 us
  Pallas kernels: 4.62 us -> 5.86 us
    all_to_all x6 -> x3, blocking collectives: 87.7 us -> 50.5 us  [exchange(): return lax.all_to_all(blocks, axes, split_axis=0, concat_axis=0, tiled=True)]
    all_to_all x0 -> x1, starting transfers between devices: none -> 10.3 us  [exchange(): return lax.all_to_all(blocks, axes, split_axis=0, concat_axis=0, tiled=True)]
    all_to_all x0 -> x1, waiting for transfers between devices: none -> 8.53 us  [exchange(): return lax.all_to_all(blocks, axes, split_axis=0, concat_axis=0, tiled=True)]
    ppermute x0 -> x2, starting transfers between devices: none -> 7.72 us  [the longest x1 5.59 us: body(): share = product(kept, came, half, lax.ppermute(half, CORE, SWAP))]
    dot_general x1 -> x0, matrix products: 2.91 us -> none  [body(): lax.dot_general(chol_vectors, amplitudes, contract, preferred_element_typ...]
    unnamed x4 -> x2, local copies, waits for them, and re-layouts: 2.12 us -> 0.01 us
    pallas_call x1 -> x3, Pallas kernels: 4.62 us -> 5.86 us  [the longest x1 4.03 us: coupling_part(): pl.pallas_call(coupling_kernel, in_specs=[IN_HBM] * 2, out_specs=[WHOLE,...]
    ppermute x0 -> x2, waiting for transfers between devices: none -> 1.13 us  [the longest x1 1.13 us: body(): share = product(kept, came, half, lax.ppermute(half, CORE, SWAP))]
  transfers between devices with their start and end apart: 0 -> 3, of which waited for: 0 -> 2; matrix products, arithmetic and copies ran while one was open for 0% -> 0% of each run, Pallas kernels for 0% -> 0%
where the time goes in v2:
time: 84.6 us; the launch traced here: 84.2 us
  blocking collectives  50.5 us (60%)
  starting transfers between devices  18 us (21%)
  waiting for transfers between devices  9.67 us (11%)
  Pallas kernels  5.86 us (7%)
    all_to_all x3, blocking collectives, exchange(): return lax.all_to_all(blocks, axes, split_axis=0, concat_axis=0, tiled=True)  50.5 us
    all_to_all x1, starting transfers between devices, exchange(): return lax.all_to_all(blocks, axes, split_axis=0, concat_axis=0, tiled=True)  10.3 us
    all_to_all x1, waiting for transfers between devices, exchange(): return lax.all_to_all(blocks, axes, split_axis=0, concat_axis=0, tiled=True)  8.53 us
    ppermute x1, starting transfers between devices, body(): share = product(kept, came, half, lax.ppermute(half, CORE, SWAP))  5.59 us
    pallas_call x1, Pallas kernels, coupling_part(): pl.pallas_call(coupling_kernel, in_specs=[IN_HBM] * 2, out_specs=[WHOLE,...  4.03 us
    ppermute x1, starting transfers between devices, body(): came = lax.ppermute(sent, YL, SWAP)  2.13 us
  transfers between devices with their start and end apart: 3, of which 2 were waited for; matrix products, arithmetic and copies ran while one was open for 0% of the time, Pallas kernels for 0%

profile of v2, /device:TPU:1, one launch (start us, length us, event | category | flops | bytes accessed | tf_op | source)
XLA Modules:
  0.0 84.2 jit_solution(17409198025602279688)
XLA Ops:
  0.0 4.0 %shard_map.37 = (bf16[256,512]{1,0:T(8,128)(2,1)}, bf16[1536,512]{1,0:T(8,128)(2,1)S(1)}, bf16[1536,512]{1,0:T(8,128)(2,1)}) custom-call(bf16[3072,512]{1,0:T(8,128)(2,1)} %l_hbm.1, bf16[3072,256]{1,0:T(8,128)(2,1)} %a_hbm.1), custom_call_target="tpu_custom_call" | custom-call | flops 805306368 | bytes 8126464 | tf_op jit(solution)/shard_map/pallas_call | solution.py:91
  4.0 10.3 %all-to-all-start = ((bf16[16,16,512]{2,1,0:T(8,128)(2,1)}), bf16[16,16,512]{2,1,0:T(8,128)(2,1)S(1)}, u32[]{:S(2)}, u32[]{:S(2)}) async-start(bf16[16,16,512]{2,1,0:T(8,128)(2,1)} %bitcast), calls=%async_computation | async-start | bytes 524288 | tf_op jit(solution)/shard_map/all_to_all | solution.py:29
  14.3 2.1 %collective-permute-start = (bf16[1536,512]{1,0:T(8,128)(2,1)}, bf16[1536,512]{1,0:T(8,128)(2,1)S(1)}, u32[]{:S(2)}, u32[]{:S(2)}) collective-permute-start(bf16[1536,512]{1,0:T(8,128)(2,1)} %get-tuple-element.9), channel_id=1, source_target_pairs={{0,1},{1,0},{2,3},{3,2},{4,5},{5,4},{6,7},{7,6},{8,9},{9,8},{10,11... | collective-permute-start | bytes 4718600 | tf_op jit(solution)/shard_map/ppermute | solution.py:170
  16.4 8.5 %all-to-all-done = bf16[16,16,512]{2,1,0:T(8,128)(2,1)S(1)} async-done(((bf16[16,16,512]{2,1,0:T(8,128)(2,1)}), bf16[16,16,512]{2,1,0:T(8,128)(2,1)S(1)}, u32[]{:S(2)}, u32[]{:S(2)}) %all-to-all-start) | async-done | bytes 262176 | tf_op jit(solution)/shard_map/all_to_all | solution.py:29
  25.0 24.2 %all_to_all.20 = bf16[4,16,512]{2,1,0:T(8,128)(2,1)S(1)} all-to-all(bf16[4,16,512]{2,1,0:T(8,128)(2,1)S(1)} %broadcast_in_dim.6), channel_id=1, replica_groups=mesh['z_far'=4,'z_near'=4,'y_hi'=2,'core'=2,'x'=4,'y_lo'=2] {'z_far'}, dimensions={0} | all-to-all | bytes 131072 | tf_op jit(solution)/shard_map/all_to_all | solution.py:29
  49.2 11.0 %all_to_all.21 = bf16[16,16,512]{2,1,0:T(8,128)(2,1)S(1)} all-to-all(bf16[16,16,512]{2,1,0:T(8,128)(2,1)S(1)} %broadcast_in_dim.7), channel_id=1, replica_groups=mesh['z_far'=4,'z_near'=4,'y_hi'=2,'core'=2,'x'=4,'y_lo'=2] {'y_lo','z_n..., dimensions={0} | all-to-all | bytes 524288 | tf_op jit(solution)/shard_map/all_to_all | solution.py:29
  60.2 5.6 %collective-permute-start.1 = (bf16[2,128,512]{2,1,0:T(8,128)(2,1)S(1)}, bf16[2,128,512]{2,1,0:T(8,128)(2,1)S(1)}, u32[]{:S(2)}, u32[]{:S(2)}) collective-permute-start(bf16[2,128,512]{2,1,0:T(8,128)(2,1)S(1)} %bitcast.2), channel_id=1, source_target_pairs={{0,8},{8,0},{1,9},{9,1},{2,10},{10,2},{3,11},{11,3},{4,12},{12,4},... | collective-permute-start | bytes 786440 | tf_op jit(solution)/shard_map/ppermute | solution.py:176
  65.8 0.0 collective-permute-done.came_ref
  65.8 1.1 %collective-permute-done.1.other_ref = bf16[2,128,512]{2,1,0:T(8,128)(2,1)S(1)} collective-permute-done((bf16[2,128,512]{2,1,0:T(8,128)(2,1)S(1)}, bf16[2,128,512]{2,1,0:T(8,128)(2,1)S(1)}, u32[]{:S(2)}, u32[]{:S(2)}) %collective-permute-start.1) | collective-permute-done | bytes 262176 | tf_op jit(solution)/shard_map/ppermute | solution.py:176
  67.0 1.0 %shard_map.38 = bf16[4,384,256]{2,1,0:T(8,128)(2,1)S(1)} custom-call(bf16[1536,512]{1,0:T(8,128)(2,1)S(1)} %get-tuple-element.8.kept_ref, bf16[1536,512]{1,0:T(8,128)(2,1)S(1)} %collective-permute-done.came_ref, bf16[2,128,512]{2,1,0:T(8,128)(2,1)S(1)} %bitcast.3, bf16[2,128,512]{2,1,0:T(8,128)(2,1)S(1)} %collective-permute-done.1.other_ref), custom_call_target="tpu_custom_call" | custom-call | flops 805306368 | bytes 4456448 | tf_op jit(solution)/shard_map/pallas_call | solution.py:133
  68.0 0.0 copy-start
  68.0 15.4 %all_to_all.22.arrived_ref = bf16[4,384,256]{2,1,0:T(8,128)(2,1)S(1)} all-to-all(bf16[4,384,256]{2,1,0:T(8,128)(2,1)S(1)} %shard_map.38), channel_id=1, replica_groups=mesh['z_far'=4,'z_near'=4,'y_hi'=2,'core'=2,'x'=4,'y_lo'=2] {'x'}, dimensions={0} | all-to-all | bytes 1572864 | tf_op jit(solution)/shard_map/all_to_all | solution.py:29
  83.4 0.0 copy-done
  83.4 0.8 shard_map.39
  (4 shorter events, 0.1 us)
Async XLA Ops:
  4.0 20.9 %all-to-all-start = ((bf16[16,16,512]{2,1,0:T(8,128)(2,1)}), bf16[16,16,512]{2,1,0:T(8,128)(2,1)S(1)}, u32[]{:S(2)}, u32[]{:S(2)}) async-start(bf16[16,16,512]{2,1,0:T(8,128)(2,1)} %bitcast), calls=%async_computation | async-start | bytes 524288 | tf_op jit(solution)/shard_map/all_to_all | solution.py:29
  14.3 51.5 %collective-permute-start = (bf16[1536,512]{1,0:T(8,128)(2,1)}, bf16[1536,512]{1,0:T(8,128)(2,1)S(1)}, u32[]{:S(2)}, u32[]{:S(2)}) collective-permute-start(bf16[1536,512]{1,0:T(8,128)(2,1)} %get-tuple-element.9), channel_id=1, source_target_pairs={{0,1},{1,0},{2,3},{3,2},{4,5},{5,4},{6,7},{7,6},{8,9},{9,8},{10,11... | collective-permute-start | bytes 4718600 | tf_op jit(solution)/shard_map/ppermute | solution.py:170
  60.2 6.7 %collective-permute-start.1 = (bf16[2,128,512]{2,1,0:T(8,128)(2,1)S(1)}, bf16[2,128,512]{2,1,0:T(8,128)(2,1)S(1)}, u32[]{:S(2)}, u32[]{:S(2)}) collective-permute-start(bf16[2,128,512]{2,1,0:T(8,128)(2,1)S(1)} %bitcast.2), channel_id=1, source_target_pairs={{0,8},{8,0},{1,9},{9,1},{2,10},{10,2},{3,11},{11,3},{4,12},{12,4},... | collective-permute-start | bytes 786440 | tf_op jit(solution)/shard_map/ppermute | solution.py:176
  68.0 15.4 %copy-start = (bf16[384,256]{1,0:T(8,128)(2,1)S(1)}, bf16[384,256]{1,0:T(8,128)(2,1)}, u32[]{:S(2)}) copy-start(bf16[384,256]{1,0:T(8,128)(2,1)} %prior_ref.1) | copy-start | bytes 589828

commit v3 on v2

--- a/solution.py
+++ b/solution.py
@@ -10,6 +10,7 @@
 SIZES = (4, 4, 2, 2, 4, 2)
 OV, VEC = (FAR, NEAR, YH, CORE), (X, YL)
 SWAP = [(0, 1), (1, 0)]
+PAIRS = ([(0, 1), (1, 0), (2, 3), (3, 2)], [(1, 2), (2, 1), (3, 0), (0, 3)])
 LIMIT = 24 << 20
 WHOLE = pl.BlockSpec(memory_space=pltpu.VMEM)
 IN_HBM = pl.BlockSpec(memory_space=pltpu.HBM)
@@ -34,7 +35,7 @@
 
 
 def summed(blocks):
-    return blocks.astype(jnp.float32).sum(axis=0).astype(jnp.bfloat16)
+    return blocks.astype(jnp.float32).sum(axis=0)
 
 
 def coupling_kernel(l_hbm, a_hbm, part_ref, kept_ref, sent_hbm, l_ref, a_ref, total_ref, l_sems, a_sems, sent_sems):
@@ -170,7 +171,9 @@
     came = lax.ppermute(sent, YL, SWAP)
     near = (CORE, NEAR, YH)
     piece = summed(exchange(part.reshape(lax.axis_size(near), -1, part.shape[-1]), near))
-    piece = summed(copies(piece, FAR))
+    for pairs in PAIRS:
+        piece += lax.ppermute(piece, FAR, pairs)
+    piece = piece.astype(jnp.bfloat16)
     half = copies(piece, (YL, NEAR, YH))
     half = half.reshape(2, -1, half.shape[-1])
     share = product(kept, came, half, lax.ppermute(half, CORE, SWAP))

time: 84.6 us -> 81.3 us (0.961)
  blocking collectives: 50.5 us -> 29.1 us
  starting transfers between devices: 18 us -> 33.6 us
  waiting for transfers between devices: 9.67 us -> 12.2 us
    all_to_all x3 -> x2, blocking collectives: 50.5 us -> 29.1 us  [exchange(): return lax.all_to_all(blocks, axes, split_axis=0, concat_axis=0, tiled=True)]
    ppermute x0 -> x2, starting transfers between devices: none -> 16.9 us  [body(): piece += lax.ppermute(piece, FAR, pairs)]
    ppermute x0 -> x2, waiting for transfers between devices: none -> 2.58 us  [body(): piece += lax.ppermute(piece, FAR, pairs)]
    ppermute x1, starting transfers between devices: 5.59 us -> 4.31 us  [body(): share = product(kept, came, half, lax.ppermute(half, CORE, SWAP))]
  transfers between devices with their start and end apart: 3 -> 5, of which waited for: 2 -> 4; matrix products, arithmetic and copies ran while one was open for 0% -> 0% of each run, Pallas kernels for 0% -> 0%
where the time goes in v3:
time: 81.3 us; the launch traced here: 80.9 us
  starting transfers between devices  33.6 us (41%)
  blocking collectives  29.1 us (36%)
  waiting for transfers between devices  12.2 us (15%)
  Pallas kernels  5.85 us (7%)
    all_to_all x2, blocking collectives, exchange(): return lax.all_to_all(blocks, axes, split_axis=0, concat_axis=0, tiled=True)  29.1 us
    ppermute x2, starting transfers between devices, body(): piece += lax.ppermute(piece, FAR, pairs)  16.9 us
    all_to_all x1, starting transfers between devices, exchange(): return lax.all_to_all(blocks, axes, split_axis=0, concat_axis=0, tiled=True)  10.3 us
    all_to_all x1, waiting for transfers between devices, exchange(): return lax.all_to_all(blocks, axes, split_axis=0, concat_axis=0, tiled=True)  8.53 us
    ppermute x1, starting transfers between devices, body(): share = product(kept, came, half, lax.ppermute(half, CORE, SWAP))  4.31 us
    pallas_call x1, Pallas kernels, coupling_part(): pl.pallas_call(coupling_kernel, in_specs=[IN_HBM] * 2, out_specs=[WHOLE,...  4.02 us
    ppermute x2, waiting for transfers between devices, body(): piece += lax.ppermute(piece, FAR, pairs)  2.58 us
    ppermute x1, starting transfers between devices, body(): came = lax.ppermute(sent, YL, SWAP)  2.13 us
  transfers between devices with their start and end apart: 5, of which 4 were waited for; matrix products, arithmetic and copies ran while one was open for 0% of the time, Pallas kernels for 0%

profile of v3, /device:TPU:1, one launch (start us, length us, event | category | flops | bytes accessed | tf_op | source)
XLA Modules:
  0.0 80.9 jit_solution(10215718810096083564)
XLA Ops:
  0.0 4.0 %shard_map.37 = (bf16[256,512]{1,0:T(8,128)(2,1)}, bf16[1536,512]{1,0:T(8,128)(2,1)S(1)}, bf16[1536,512]{1,0:T(8,128)(2,1)}) custom-call(bf16[3072,512]{1,0:T(8,128)(2,1)} %l_hbm.1, bf16[3072,256]{1,0:T(8,128)(2,1)} %a_hbm.1), custom_call_target="tpu_custom_call" | custom-call | flops 805306368 | bytes 8126464 | tf_op jit(solution)/shard_map/pallas_call | solution.py:92
  4.0 10.3 %all-to-all-start = ((bf16[16,16,512]{2,1,0:T(8,128)(2,1)}), bf16[16,16,512]{2,1,0:T(8,128)(2,1)S(1)}, u32[]{:S(2)}, u32[]{:S(2)}) async-start(bf16[16,16,512]{2,1,0:T(8,128)(2,1)} %bitcast), calls=%async_computation | async-start | bytes 524288 | tf_op jit(solution)/shard_map/all_to_all | solution.py:30
  14.3 2.1 %collective-permute-start = (bf16[1536,512]{1,0:T(8,128)(2,1)}, bf16[1536,512]{1,0:T(8,128)(2,1)S(1)}, u32[]{:S(2)}, u32[]{:S(2)}) collective-permute-start(bf16[1536,512]{1,0:T(8,128)(2,1)} %get-tuple-element.9), channel_id=1, source_target_pairs={{0,1},{1,0},{2,3},{3,2},{4,5},{5,4},{6,7},{7,6},{8,9},{9,8},{10,11... | collective-permute-start | bytes 4718600 | tf_op jit(solution)/shard_map/ppermute | solution.py:171
  16.4 8.5 %all-to-all-done = bf16[16,16,512]{2,1,0:T(8,128)(2,1)S(1)} async-done(((bf16[16,16,512]{2,1,0:T(8,128)(2,1)}), bf16[16,16,512]{2,1,0:T(8,128)(2,1)S(1)}, u32[]{:S(2)}, u32[]{:S(2)}) %all-to-all-start) | async-done | bytes 262176 | tf_op jit(solution)/shard_map/all_to_all | solution.py:30
  25.0 8.7 %collective-permute-start.1 = (f32[16,512]{1,0:T(8,128)S(1)}, f32[16,512]{1,0:T(8,128)S(1)}, u32[]{:S(2)}, u32[]{:S(2)}) collective-permute-start(f32[16,512]{1,0:T(8,128)S(1)} %convert_reduce_fusion), channel_id=1, source_target_pairs={{0,128},{128,0},{256,384},{384,256},{1,129},{129,1},{257,385},{385... | collective-permute-start | bytes 98312 | tf_op jit(solution)/shard_map/ppermute | solution.py:175
  33.7 1.3 %collective-permute-done.1 = f32[16,512]{1,0:T(8,128)S(1)} collective-permute-done((f32[16,512]{1,0:T(8,128)S(1)}, f32[16,512]{1,0:T(8,128)S(1)}, u32[]{:S(2)}, u32[]{:S(2)}) %collective-permute-start.1) | collective-permute-done | bytes 32800 | tf_op jit(solution)/shard_map/ppermute | solution.py:175
  35.0 8.2 %collective-permute-start.2 = (f32[16,512]{1,0:T(8,128)S(1)}, f32[16,512]{1,0:T(8,128)S(1)}, u32[]{:S(2)}, u32[]{:S(2)}) collective-permute-start(f32[16,512]{1,0:T(8,128)S(1)} %add.6), channel_id=1, source_target_pairs={{128,256},{256,128},{384,0},{0,384},{129,257},{257,129},{385,1},{1... | collective-permute-start | bytes 98312 | tf_op jit(solution)/shard_map/ppermute | solution.py:175
  43.2 1.3 %collective-permute-done.2 = f32[16,512]{1,0:T(8,128)S(1)} collective-permute-done((f32[16,512]{1,0:T(8,128)S(1)}, f32[16,512]{1,0:T(8,128)S(1)}, u32[]{:S(2)}, u32[]{:S(2)}) %collective-permute-start.2) | collective-permute-done | bytes 32800 | tf_op jit(solution)/shard_map/ppermute | solution.py:175
  44.5 13.7 %all_to_all.15 = bf16[16,16,512]{2,1,0:T(8,128)(2,1)S(1)} all-to-all(bf16[16,16,512]{2,1,0:T(8,128)(2,1)S(1)} %broadcast_in_dim.3), channel_id=1, replica_groups=mesh['z_far'=4,'z_near'=4,'y_hi'=2,'core'=2,'x'=4,'y_lo'=2] {'y_lo','z_n..., dimensions={0} | all-to-all | bytes 524288 | tf_op jit(solution)/shard_map/all_to_all | solution.py:30
  58.2 4.3 %collective-permute-start.3 = (bf16[2,128,512]{2,1,0:T(8,128)(2,1)S(1)}, bf16[2,128,512]{2,1,0:T(8,128)(2,1)S(1)}, u32[]{:S(2)}, u32[]{:S(2)}) collective-permute-start(bf16[2,128,512]{2,1,0:T(8,128)(2,1)S(1)} %bitcast.2), channel_id=1, source_target_pairs={{0,8},{8,0},{1,9},{9,1},{2,10},{10,2},{3,11},{11,3},{4,12},{12,4},... | collective-permute-start | bytes 786440 | tf_op jit(solution)/shard_map/ppermute | solution.py:179
  62.5 0.0 collective-permute-done.came_ref
  62.5 1.1 %collective-permute-done.3.other_ref = bf16[2,128,512]{2,1,0:T(8,128)(2,1)S(1)} collective-permute-done((bf16[2,128,512]{2,1,0:T(8,128)(2,1)S(1)}, bf16[2,128,512]{2,1,0:T(8,128)(2,1)S(1)}, u32[]{:S(2)}, u32[]{:S(2)}) %collective-permute-start.3) | collective-permute-done | bytes 262176 | tf_op jit(solution)/shard_map/ppermute | solution.py:179
  63.7 1.0 %shard_map.38 = bf16[4,384,256]{2,1,0:T(8,128)(2,1)S(1)} custom-call(bf16[1536,512]{1,0:T(8,128)(2,1)S(1)} %get-tuple-element.8.kept_ref, bf16[1536,512]{1,0:T(8,128)(2,1)S(1)} %collective-permute-done.came_ref, bf16[2,128,512]{2,1,0:T(8,128)(2,1)S(1)} %bitcast.3, bf16[2,128,512]{2,1,0:T(8,128)(2,1)S(1)} %collective-permute-done.3.other_ref), custom_call_target="tpu_custom_call" | custom-call | flops 805306368 | bytes 4456448 | tf_op jit(solution)/shard_map/pallas_call | solution.py:134
  64.7 0.0 copy-start
  64.7 15.4 %all_to_all.16.arrived_ref = bf16[4,384,256]{2,1,0:T(8,128)(2,1)S(1)} all-to-all(bf16[4,384,256]{2,1,0:T(8,128)(2,1)S(1)} %shard_map.38), channel_id=1, replica_groups=mesh['z_far'=4,'z_near'=4,'y_hi'=2,'core'=2,'x'=4,'y_lo'=2] {'x'}, dimensions={0} | all-to-all | bytes 1572864 | tf_op jit(solution)/shard_map/all_to_all | solution.py:30
  80.1 0.0 copy-done
  80.1 0.8 shard_map.39
  (4 shorter events, 0.1 us)
Async XLA Ops:
  4.0 20.9 %all-to-all-start = ((bf16[16,16,512]{2,1,0:T(8,128)(2,1)}), bf16[16,16,512]{2,1,0:T(8,128)(2,1)S(1)}, u32[]{:S(2)}, u32[]{:S(2)}) async-start(bf16[16,16,512]{2,1,0:T(8,128)(2,1)} %bitcast), calls=%async_computation | async-start | bytes 524288 | tf_op jit(solution)/shard_map/all_to_all | solution.py:30
  14.3 48.3 %collective-permute-start = (bf16[1536,512]{1,0:T(8,128)(2,1)}, bf16[1536,512]{1,0:T(8,128)(2,1)S(1)}, u32[]{:S(2)}, u32[]{:S(2)}) collective-permute-start(bf16[1536,512]{1,0:T(8,128)(2,1)} %get-tuple-element.9), channel_id=1, source_target_pairs={{0,1},{1,0},{2,3},{3,2},{4,5},{5,4},{6,7},{7,6},{8,9},{9,8},{10,11... | collective-permute-start | bytes 4718600 | tf_op jit(solution)/shard_map/ppermute | solution.py:171
  25.0 10.0 %collective-permute-start.1 = (f32[16,512]{1,0:T(8,128)S(1)}, f32[16,512]{1,0:T(8,128)S(1)}, u32[]{:S(2)}, u32[]{:S(2)}) collective-permute-start(f32[16,512]{1,0:T(8,128)S(1)} %convert_reduce_fusion), channel_id=1, source_target_pairs={{0,128},{128,0},{256,384},{384,256},{1,129},{129,1},{257,385},{385... | collective-permute-start | bytes 98312 | tf_op jit(solution)/shard_map/ppermute | solution.py:175
  35.0 9.5 %collective-permute-start.2 = (f32[16,512]{1,0:T(8,128)S(1)}, f32[16,512]{1,0:T(8,128)S(1)}, u32[]{:S(2)}, u32[]{:S(2)}) collective-permute-start(f32[16,512]{1,0:T(8,128)S(1)} %add.6), channel_id=1, source_target_pairs={{128,256},{256,128},{384,0},{0,384},{129,257},{257,129},{385,1},{1... | collective-permute-start | bytes 98312 | tf_op jit(solution)/shard_map/ppermute | solution.py:175
  58.2 5.5 %collective-permute-start.3 = (bf16[2,128,512]{2,1,0:T(8,128)(2,1)S(1)}, bf16[2,128,512]{2,1,0:T(8,128)(2,1)S(1)}, u32[]{:S(2)}, u32[]{:S(2)}) collective-permute-start(bf16[2,128,512]{2,1,0:T(8,128)(2,1)S(1)} %bitcast.2), channel_id=1, source_target_pairs={{0,8},{8,0},{1,9},{9,1},{2,10},{10,2},{3,11},{11,3},{4,12},{12,4},... | collective-permute-start | bytes 786440 | tf_op jit(solution)/shard_map/ppermute | solution.py:179
  64.7 15.4 %copy-start = (bf16[384,256]{1,0:T(8,128)(2,1)S(1)}, bf16[384,256]{1,0:T(8,128)(2,1)}, u32[]{:S(2)}) copy-start(bf16[384,256]{1,0:T(8,128)(2,1)} %prior_ref.1) | copy-start | bytes 589828

commit v4 on v3

--- a/solution.py
+++ b/solution.py
@@ -6,9 +6,10 @@
 from jax.sharding import Mesh
 from jax.sharding import PartitionSpec as P
 
-FAR, NEAR, YH, CORE, X, YL = "z_far", "z_near", "y_hi", "core", "x", "y_lo"
-SIZES = (4, 4, 2, 2, 4, 2)
-OV, VEC = (FAR, NEAR, YH, CORE), (X, YL)
+FAR, NEAR, YH, CORE, YL = "z_far", "z_near", "y_hi", "core", "y_lo"
+X = ("x_hi", "x_lo")
+SIZES = (4, 4, 2, 2, 2, 2, 2)
+OV, VEC = (FAR, NEAR, YH, CORE), (*X, YL)
 SWAP = [(0, 1), (1, 0)]
 PAIRS = ([(0, 1), (1, 0), (2, 3), (3, 2)], [(1, 2), (2, 1), (3, 0), (0, 3)])
 LIMIT = 24 << 20
@@ -114,9 +115,10 @@
 def product_kernel(kept_ref, came_ref, own_ref, other_ref, out_ref, c_ref):
     mine, core = lax.axis_index(YL), lax.axis_index(CORE)
     blocks, size, _ = out_ref.shape
-    half = own_ref.shape[1]
+    parts, _, part, _ = own_ref.shape
     for at, ref in ((core, own_ref), (1 - core, other_ref)):
-        c_ref[:, pl.ds(pl.multiple_of(at * half, half), half), :] = ref[...]
+        for k in range(parts):
+            c_ref[:, pl.ds(pl.multiple_of((at * parts + k) * part, part), part), :] = ref[k]
     own, other = c_ref[mine], c_ref[1 - mine]
 
     def by(x, coupling):
@@ -124,19 +126,19 @@
 
     for k in range(blocks):
         rows = pl.ds(k * size, size)
-        out_ref[k] = (by(kept_ref[rows], own) + by(came_ref[rows], other)).astype(jnp.bfloat16)
+        out_ref[2 * (k % 2) + k // 2] = (by(kept_ref[rows], own) + by(came_ref[rows], other)).astype(jnp.bfloat16)
 
 
 def product(kept, came, own, other):
     rows, depth = kept.shape
-    cols = 2 * own.shape[1]
+    cols = 2 * own.shape[0] * own.shape[2]
     blocks = lax.axis_size(X)
     return pl.pallas_call(
         product_kernel,
         in_specs=[WHOLE] * 4,
         out_specs=WHOLE,
         out_shape=jax.ShapeDtypeStruct((blocks, rows // blocks, cols), jnp.bfloat16),
-        scratch_shapes=[pltpu.VMEM((2, cols, depth), jnp.bfloat16)],
+        scratch_shapes=[pltpu.VMEM((own.shape[1], cols, depth), jnp.bfloat16)],
         compiler_params=pltpu.CompilerParams(vmem_limit_bytes=LIMIT),
         cost_estimate=pl.CostEstimate(
             flops=4 * kept.size * cols,
@@ -169,15 +171,15 @@
 def body(chol_vectors, amplitudes, sigma_prior):
     part, kept, sent = coupling_part(chol_vectors, amplitudes)
     came = lax.ppermute(sent, YL, SWAP)
-    near = (CORE, NEAR, YH)
+    near = (CORE, YH, NEAR)
     piece = summed(exchange(part.reshape(lax.axis_size(near), -1, part.shape[-1]), near))
     for pairs in PAIRS:
         piece += lax.ppermute(piece, FAR, pairs)
     piece = piece.astype(jnp.bfloat16)
-    half = copies(piece, (YL, NEAR, YH))
-    half = half.reshape(2, -1, half.shape[-1])
+    half = copies(piece, (YH, YL, NEAR))
+    half = half.reshape(lax.axis_size(YH), lax.axis_size(YL), -1, half.shape[-1])
     share = product(kept, came, half, lax.ppermute(half, CORE, SWAP))
-    return finish(exchange(share, X), sigma_prior)
+    return finish(exchange(share, X[::-1]), sigma_prior)
 
 
 def solution(mesh):

time: 81.3 us -> 81.3 us (level)
  waiting for transfers between devices: 12.2 us -> 15.8 us
  blocking collectives: 29.1 us -> 26.8 us
  starting transfers between devices: 33.6 us -> 32.3 us
    ppermute x2, waiting for transfers between devices: 2.58 us -> 5.21 us  [body(): piece += lax.ppermute(piece, FAR, pairs)]
    all_to_all x2, blocking collectives: 29.1 us -> 26.8 us  [exchange(): return lax.all_to_all(blocks, axes, split_axis=0, concat_axis=0, tiled=True)]
    ppermute x2, starting transfers between devices: 16.9 us -> 15.1 us  [body(): piece += lax.ppermute(piece, FAR, pairs)]
    all_to_all x1, waiting for transfers between devices: 8.53 us -> 9.43 us  [exchange(): return lax.all_to_all(blocks, axes, split_axis=0, concat_axis=0, tiled=True)]
where the time goes in v4:
time: 81.3 us; the launch traced here: 80.9 us
  starting transfers between devices  32.3 us (40%)
  blocking collectives  26.8 us (33%)
  waiting for transfers between devices  15.8 us (19%)
  Pallas kernels  5.86 us (7%)
    all_to_all x2, blocking collectives, exchange(): return lax.all_to_all(blocks, axes, split_axis=0, concat_axis=0, tiled=True)  26.8 us
    ppermute x2, starting transfers between devices, body(): piece += lax.ppermute(piece, FAR, pairs)  15.1 us
    all_to_all x1, starting transfers between devices, exchange(): return lax.all_to_all(blocks, axes, split_axis=0, concat_axis=0, tiled=True)  10.3 us
    all_to_all x1, waiting for transfers between devices, exchange(): return lax.all_to_all(blocks, axes, split_axis=0, concat_axis=0, tiled=True)  9.43 us
    ppermute x2, waiting for transfers between devices, body(): piece += lax.ppermute(piece, FAR, pairs)  5.21 us
    ppermute x1, starting transfers between devices, body(): share = product(kept, came, half, lax.ppermute(half, CORE, SWAP))  4.81 us
    pallas_call x1, Pallas kernels, coupling_part(): pl.pallas_call(coupling_kernel, in_specs=[IN_HBM] * 2, out_specs=[WHOLE,...  4.02 us
    ppermute x1, starting transfers between devices, body(): came = lax.ppermute(sent, YL, SWAP)  2.13 us
  transfers between devices with their start and end apart: 5, of which 4 were waited for; matrix products, arithmetic and copies ran while one was open for 0% of the time, Pallas kernels for 0%

profile of v4, /device:TPU:1, one launch (start us, length us, event | category | flops | bytes accessed | tf_op | source)
XLA Modules:
  0.0 80.9 jit_solution(1413989895916905519)
XLA Ops:
  0.0 4.0 %shard_map.37 = (bf16[256,512]{1,0:T(8,128)(2,1)}, bf16[1536,512]{1,0:T(8,128)(2,1)S(1)}, bf16[1536,512]{1,0:T(8,128)(2,1)}) custom-call(bf16[3072,512]{1,0:T(8,128)(2,1)} %l_hbm.1, bf16[3072,256]{1,0:T(8,128)(2,1)} %a_hbm.1), custom_call_target="tpu_custom_call" | custom-call | flops 805306368 | bytes 8126464 | tf_op jit(solution)/shard_map/pallas_call | solution.py:93
  4.0 10.3 %all-to-all-start = ((bf16[16,16,512]{2,1,0:T(8,128)(2,1)}), bf16[16,16,512]{2,1,0:T(8,128)(2,1)S(1)}, u32[]{:S(2)}, u32[]{:S(2)}) async-start(bf16[16,16,512]{2,1,0:T(8,128)(2,1)} %bitcast), calls=%async_computation | async-start | bytes 524288 | tf_op jit(solution)/shard_map/all_to_all | solution.py:31
  14.3 2.1 %collective-permute-start = (bf16[1536,512]{1,0:T(8,128)(2,1)}, bf16[1536,512]{1,0:T(8,128)(2,1)S(1)}, u32[]{:S(2)}, u32[]{:S(2)}) collective-permute-start(bf16[1536,512]{1,0:T(8,128)(2,1)} %get-tuple-element.9), channel_id=1, source_target_pairs={{0,1},{1,0},{2,3},{3,2},{4,5},{5,4},{6,7},{7,6},{8,9},{9,8},{10,11... | collective-permute-start | bytes 4718600 | tf_op jit(solution)/shard_map/ppermute | solution.py:173
  16.4 9.4 %all-to-all-done = bf16[16,16,512]{2,1,0:T(8,128)(2,1)S(1)} async-done(((bf16[16,16,512]{2,1,0:T(8,128)(2,1)}), bf16[16,16,512]{2,1,0:T(8,128)(2,1)S(1)}, u32[]{:S(2)}, u32[]{:S(2)}) %all-to-all-start) | async-done | bytes 262176 | tf_op jit(solution)/shard_map/all_to_all | solution.py:31
  25.9 8.6 %collective-permute-start.1 = (f32[16,512]{1,0:T(8,128)S(1)}, f32[16,512]{1,0:T(8,128)S(1)}, u32[]{:S(2)}, u32[]{:S(2)}) collective-permute-start(f32[16,512]{1,0:T(8,128)S(1)} %convert_reduce_fusion), channel_id=1, source_target_pairs={{0,128},{128,0},{256,384},{384,256},{1,129},{129,1},{257,385},{385... | collective-permute-start | bytes 98312 | tf_op jit(solution)/shard_map/ppermute | solution.py:177
  34.6 3.1 %collective-permute-done.1 = f32[16,512]{1,0:T(8,128)S(1)} collective-permute-done((f32[16,512]{1,0:T(8,128)S(1)}, f32[16,512]{1,0:T(8,128)S(1)}, u32[]{:S(2)}, u32[]{:S(2)}) %collective-permute-start.1) | collective-permute-done | bytes 32800 | tf_op jit(solution)/shard_map/ppermute | solution.py:177
  37.7 6.5 %collective-permute-start.2 = (f32[16,512]{1,0:T(8,128)S(1)}, f32[16,512]{1,0:T(8,128)S(1)}, u32[]{:S(2)}, u32[]{:S(2)}) collective-permute-start(f32[16,512]{1,0:T(8,128)S(1)} %add.6), channel_id=1, source_target_pairs={{128,256},{256,128},{384,0},{0,384},{129,257},{257,129},{385,1},{1... | collective-permute-start | bytes 98312 | tf_op jit(solution)/shard_map/ppermute | solution.py:177
  44.2 2.1 %collective-permute-done.2 = f32[16,512]{1,0:T(8,128)S(1)} collective-permute-done((f32[16,512]{1,0:T(8,128)S(1)}, f32[16,512]{1,0:T(8,128)S(1)}, u32[]{:S(2)}, u32[]{:S(2)}) %collective-permute-start.2) | collective-permute-done | bytes 32800 | tf_op jit(solution)/shard_map/ppermute | solution.py:177
  46.3 11.7 %all_to_all.15 = bf16[16,16,512]{2,1,0:T(8,128)(2,1)S(1)} all-to-all(bf16[16,16,512]{2,1,0:T(8,128)(2,1)S(1)} %broadcast_in_dim.3), channel_id=1, replica_groups=mesh['z_far'=4,'z_near'=4,'y_hi'=2,'core'=2,'x_hi'=2,'x_lo'=2,'y_lo'=2] ..., dimensions={0} | all-to-all | bytes 524288 | tf_op jit(solution)/shard_map/all_to_all | solution.py:31
  58.0 4.8 %collective-permute-start.3 = (bf16[2,2,64,512]{3,2,1,0:T(8,128)(2,1)S(1)}, bf16[2,2,64,512]{3,2,1,0:T(8,128)(2,1)S(1)}, u32[]{:S(2)}, u32[]{:S(2)}) collective-permute-start(bf16[2,2,64,512]{3,2,1,0:T(8,128)(2,1)S(1)} %bitcast.2), channel_id=1, source_target_pairs={{0,8},{8,0},{1,9},{9,1},{2,10},{10,2},{3,11},{11,3},{4,12},{12,4},... | collective-permute-start | bytes 786440 | tf_op jit(solution)/shard_map/ppermute | solution.py:181
  62.8 0.0 collective-permute-done.came_ref
  62.8 1.1 %collective-permute-done.3.other_ref = bf16[2,2,64,512]{3,2,1,0:T(8,128)(2,1)S(1)} collective-permute-done((bf16[2,2,64,512]{3,2,1,0:T(8,128)(2,1)S(1)}, bf16[2,2,64,512]{3,2,1,0:T(8,128)(2,1)S(1)}, u32[]{:S(2)}, u32[]{:S(2)}) %collective-permute-start.3) | collective-permute-done | bytes 262176 | tf_op jit(solution)/shard_map/ppermute | solution.py:181
  63.9 1.0 %shard_map.38 = bf16[4,384,256]{2,1,0:T(8,128)(2,1)S(1)} custom-call(bf16[1536,512]{1,0:T(8,128)(2,1)S(1)} %get-tuple-element.8.kept_ref, bf16[1536,512]{1,0:T(8,128)(2,1)S(1)} %collective-permute-done.came_ref, bf16[2,2,64,512]{3,2,1,0:T(8,128)(2,1)S(1)} %bitcast.3, bf16[2,2,64,512]{3,2,1,0:T(8,128)(2,1)S(1)} %collective-permute-done.3.other_ref), custom_call_target="tpu_custom_call" | custom-call | flops 805306368 | bytes 4456448 | tf_op jit(solution)/shard_map/pallas_call | solution.py:136
  65.0 0.0 copy-start
  65.0 15.1 %all_to_all.16.arrived_ref = bf16[4,384,256]{2,1,0:T(8,128)(2,1)S(1)} all-to-all(bf16[4,384,256]{2,1,0:T(8,128)(2,1)S(1)} %shard_map.38), channel_id=1, replica_groups=mesh['z_far'=4,'z_near'=4,'y_hi'=2,'core'=2,'x_hi'=2,'x_lo'=2,'y_lo'=2] ..., dimensions={0} | all-to-all | bytes 1572864 | tf_op jit(solution)/shard_map/all_to_all | solution.py:31
  80.1 0.0 copy-done
  80.1 0.8 shard_map.39
  (4 shorter events, 0.1 us)
Async XLA Ops:
  4.0 21.8 %all-to-all-start = ((bf16[16,16,512]{2,1,0:T(8,128)(2,1)}), bf16[16,16,512]{2,1,0:T(8,128)(2,1)S(1)}, u32[]{:S(2)}, u32[]{:S(2)}) async-start(bf16[16,16,512]{2,1,0:T(8,128)(2,1)} %bitcast), calls=%async_computation | async-start | bytes 524288 | tf_op jit(solution)/shard_map/all_to_all | solution.py:31
  14.3 48.5 %collective-permute-start = (bf16[1536,512]{1,0:T(8,128)(2,1)}, bf16[1536,512]{1,0:T(8,128)(2,1)S(1)}, u32[]{:S(2)}, u32[]{:S(2)}) collective-permute-start(bf16[1536,512]{1,0:T(8,128)(2,1)} %get-tuple-element.9), channel_id=1, source_target_pairs={{0,1},{1,0},{2,3},{3,2},{4,5},{5,4},{6,7},{7,6},{8,9},{9,8},{10,11... | collective-permute-start | bytes 4718600 | tf_op jit(solution)/shard_map/ppermute | solution.py:173
  25.9 11.8 %collective-permute-start.1 = (f32[16,512]{1,0:T(8,128)S(1)}, f32[16,512]{1,0:T(8,128)S(1)}, u32[]{:S(2)}, u32[]{:S(2)}) collective-permute-start(f32[16,512]{1,0:T(8,128)S(1)} %convert_reduce_fusion), channel_id=1, source_target_pairs={{0,128},{128,0},{256,384},{384,256},{1,129},{129,1},{257,385},{385... | collective-permute-start | bytes 98312 | tf_op jit(solution)/shard_map/ppermute | solution.py:177
  37.7 8.6 %collective-permute-start.2 = (f32[16,512]{1,0:T(8,128)S(1)}, f32[16,512]{1,0:T(8,128)S(1)}, u32[]{:S(2)}, u32[]{:S(2)}) collective-permute-start(f32[16,512]{1,0:T(8,128)S(1)} %add.6), channel_id=1, source_target_pairs={{128,256},{256,128},{384,0},{0,384},{129,257},{257,129},{385,1},{1... | collective-permute-start | bytes 98312 | tf_op jit(solution)/shard_map/ppermute | solution.py:177
  58.0 6.0 %collective-permute-start.3 = (bf16[2,2,64,512]{3,2,1,0:T(8,128)(2,1)S(1)}, bf16[2,2,64,512]{3,2,1,0:T(8,128)(2,1)S(1)}, u32[]{:S(2)}, u32[]{:S(2)}) collective-permute-start(bf16[2,2,64,512]{3,2,1,0:T(8,128)(2,1)S(1)} %bitcast.2), channel_id=1, source_target_pairs={{0,8},{8,0},{1,9},{9,1},{2,10},{10,2},{3,11},{11,3},{4,12},{12,4},... | collective-permute-start | bytes 786440 | tf_op jit(solution)/shard_map/ppermute | solution.py:181
  65.0 15.1 %copy-start = (bf16[384,256]{1,0:T(8,128)(2,1)S(1)}, bf16[384,256]{1,0:T(8,128)(2,1)}, u32[]{:S(2)}) copy-start(bf16[384,256]{1,0:T(8,128)(2,1)} %prior_ref.1) | copy-start | bytes 589828

commit v5 on v3

--- a/solution.py
+++ b/solution.py
@@ -10,7 +10,10 @@
 SIZES = (4, 4, 2, 2, 4, 2)
 OV, VEC = (FAR, NEAR, YH, CORE), (X, YL)
 SWAP = [(0, 1), (1, 0)]
-PAIRS = ([(0, 1), (1, 0), (2, 3), (3, 2)], [(1, 2), (2, 1), (3, 0), (0, 3)])
+RING = ([(0, 1), (1, 0), (2, 3), (3, 2)], [(1, 2), (2, 1), (3, 0), (0, 3)])
+PAIRS = [
+    [(2 * i + core, 2 * j + core) for core in (0, 1) for i, j in RING[step ^ (1 - core)]] for step in (0, 1)
+]
 LIMIT = 24 << 20
 WHOLE = pl.BlockSpec(memory_space=pltpu.VMEM)
 IN_HBM = pl.BlockSpec(memory_space=pltpu.HBM)
@@ -172,7 +175,7 @@
     near = (CORE, NEAR, YH)
     piece = summed(exchange(part.reshape(lax.axis_size(near), -1, part.shape[-1]), near))
     for pairs in PAIRS:
-        piece += lax.ppermute(piece, FAR, pairs)
+        piece += lax.ppermute(piece, (FAR, CORE), pairs)
     piece = piece.astype(jnp.bfloat16)
     half = copies(piece, (YL, NEAR, YH))
     half = half.reshape(2, -1, half.shape[-1])

time: 81.3 us -> 80.8 us (level)
  no operation moved by 1% of the time
where the time goes in v5:
time: 80.8 us; the launch traced here: 80.4 us
  starting transfers between devices  32.9 us (41%)
  blocking collectives  29.1 us (36%)
  waiting for transfers between devices  12.4 us (15%)
  Pallas kernels  5.85 us (7%)
    all_to_all x2, blocking collectives, exchange(): return lax.all_to_all(blocks, axes, split_axis=0, concat_axis=0, tiled=True)  29.1 us
    ppermute x2, starting transfers between devices, body(): piece += lax.ppermute(piece, (FAR, CORE), pairs)  16.7 us
    all_to_all x1, starting transfers between devices, exchange(): return lax.all_to_all(blocks, axes, split_axis=0, concat_axis=0, tiled=True)  10.3 us
    all_to_all x1, waiting for transfers between devices, exchange(): return lax.all_to_all(blocks, axes, split_axis=0, concat_axis=0, tiled=True)  8.53 us
    pallas_call x1, Pallas kernels, coupling_part(): pl.pallas_call(coupling_kernel, in_specs=[IN_HBM] * 2, out_specs=[WHOLE,...  4.02 us
    ppermute x1, starting transfers between devices, body(): share = product(kept, came, half, lax.ppermute(half, CORE, SWAP))  3.84 us
    ppermute x2, waiting for transfers between devices, body(): piece += lax.ppermute(piece, (FAR, CORE), pairs)  2.74 us
    ppermute x1, starting transfers between devices, body(): came = lax.ppermute(sent, YL, SWAP)  2.13 us
  transfers between devices with their start and end apart: 5, of which 4 were waited for; matrix products, arithmetic and copies ran while one was open for 0% of the time, Pallas kernels for 0%

profile of v5, /device:TPU:1, one launch (start us, length us, event | category | flops | bytes accessed | tf_op | source)
XLA Modules:
  0.0 80.4 jit_solution(18368003535496930220)
XLA Ops:
  0.0 4.0 %shard_map.37 = (bf16[256,512]{1,0:T(8,128)(2,1)}, bf16[1536,512]{1,0:T(8,128)(2,1)S(1)}, bf16[1536,512]{1,0:T(8,128)(2,1)}) custom-call(bf16[3072,512]{1,0:T(8,128)(2,1)} %l_hbm.1, bf16[3072,256]{1,0:T(8,128)(2,1)} %a_hbm.1), custom_call_target="tpu_custom_call" | custom-call | flops 805306368 | bytes 8126464 | tf_op jit(solution)/shard_map/pallas_call | solution.py:95
  4.0 10.3 %all-to-all-start = ((bf16[16,16,512]{2,1,0:T(8,128)(2,1)}), bf16[16,16,512]{2,1,0:T(8,128)(2,1)S(1)}, u32[]{:S(2)}, u32[]{:S(2)}) async-start(bf16[16,16,512]{2,1,0:T(8,128)(2,1)} %bitcast), calls=%async_computation | async-start | bytes 524288 | tf_op jit(solution)/shard_map/all_to_all | solution.py:33
  14.3 2.1 %collective-permute-start = (bf16[1536,512]{1,0:T(8,128)(2,1)}, bf16[1536,512]{1,0:T(8,128)(2,1)S(1)}, u32[]{:S(2)}, u32[]{:S(2)}) collective-permute-start(bf16[1536,512]{1,0:T(8,128)(2,1)} %get-tuple-element.9), channel_id=1, source_target_pairs={{0,1},{1,0},{2,3},{3,2},{4,5},{5,4},{6,7},{7,6},{8,9},{9,8},{10,11... | collective-permute-start | bytes 4718600 | tf_op jit(solution)/shard_map/ppermute | solution.py:174
  16.4 8.5 %all-to-all-done = bf16[16,16,512]{2,1,0:T(8,128)(2,1)S(1)} async-done(((bf16[16,16,512]{2,1,0:T(8,128)(2,1)}), bf16[16,16,512]{2,1,0:T(8,128)(2,1)S(1)}, u32[]{:S(2)}, u32[]{:S(2)}) %all-to-all-start) | async-done | bytes 262176 | tf_op jit(solution)/shard_map/all_to_all | solution.py:33
  25.0 8.7 %collective-permute-start.1 = (f32[16,512]{1,0:T(8,128)S(1)}, f32[16,512]{1,0:T(8,128)S(1)}, u32[]{:S(2)}, u32[]{:S(2)}) collective-permute-start(f32[16,512]{1,0:T(8,128)S(1)} %convert_reduce_fusion), channel_id=1, source_target_pairs={{128,256},{256,128},{384,0},{0,384},{8,136},{136,8},{264,392},{392... | collective-permute-start | bytes 98312 | tf_op jit(solution)/shard_map/ppermute | solution.py:178
  33.7 1.4 %collective-permute-done.1 = f32[16,512]{1,0:T(8,128)S(1)} collective-permute-done((f32[16,512]{1,0:T(8,128)S(1)}, f32[16,512]{1,0:T(8,128)S(1)}, u32[]{:S(2)}, u32[]{:S(2)}) %collective-permute-start.1) | collective-permute-done | bytes 32800 | tf_op jit(solution)/shard_map/ppermute | solution.py:178
  35.1 8.0 %collective-permute-start.2 = (f32[16,512]{1,0:T(8,128)S(1)}, f32[16,512]{1,0:T(8,128)S(1)}, u32[]{:S(2)}, u32[]{:S(2)}) collective-permute-start(f32[16,512]{1,0:T(8,128)S(1)} %add.6), channel_id=1, source_target_pairs={{0,128},{128,0},{256,384},{384,256},{136,264},{264,136},{392,8},{8... | collective-permute-start | bytes 98312 | tf_op jit(solution)/shard_map/ppermute | solution.py:178
  43.2 1.3 %collective-permute-done.2 = f32[16,512]{1,0:T(8,128)S(1)} collective-permute-done((f32[16,512]{1,0:T(8,128)S(1)}, f32[16,512]{1,0:T(8,128)S(1)}, u32[]{:S(2)}, u32[]{:S(2)}) %collective-permute-start.2) | collective-permute-done | bytes 32800 | tf_op jit(solution)/shard_map/ppermute | solution.py:178
  44.5 13.7 %all_to_all.15 = bf16[16,16,512]{2,1,0:T(8,128)(2,1)S(1)} all-to-all(bf16[16,16,512]{2,1,0:T(8,128)(2,1)S(1)} %broadcast_in_dim.3), channel_id=1, replica_groups=mesh['z_far'=4,'z_near'=4,'y_hi'=2,'core'=2,'x'=4,'y_lo'=2] {'y_lo','z_n..., dimensions={0} | all-to-all | bytes 524288 | tf_op jit(solution)/shard_map/all_to_all | solution.py:33
  58.2 3.8 %collective-permute-start.3 = (bf16[2,128,512]{2,1,0:T(8,128)(2,1)S(1)}, bf16[2,128,512]{2,1,0:T(8,128)(2,1)S(1)}, u32[]{:S(2)}, u32[]{:S(2)}) collective-permute-start(bf16[2,128,512]{2,1,0:T(8,128)(2,1)S(1)} %bitcast.2), channel_id=1, source_target_pairs={{0,8},{8,0},{1,9},{9,1},{2,10},{10,2},{3,11},{11,3},{4,12},{12,4},... | collective-permute-start | bytes 786440 | tf_op jit(solution)/shard_map/ppermute | solution.py:182
  62.1 0.0 collective-permute-done.came_ref
  62.1 1.1 %collective-permute-done.3.other_ref = bf16[2,128,512]{2,1,0:T(8,128)(2,1)S(1)} collective-permute-done((bf16[2,128,512]{2,1,0:T(8,128)(2,1)S(1)}, bf16[2,128,512]{2,1,0:T(8,128)(2,1)S(1)}, u32[]{:S(2)}, u32[]{:S(2)}) %collective-permute-start.3) | collective-permute-done | bytes 262176 | tf_op jit(solution)/shard_map/ppermute | solution.py:182
  63.2 1.0 %shard_map.38 = bf16[4,384,256]{2,1,0:T(8,128)(2,1)S(1)} custom-call(bf16[1536,512]{1,0:T(8,128)(2,1)S(1)} %get-tuple-element.8.kept_ref, bf16[1536,512]{1,0:T(8,128)(2,1)S(1)} %collective-permute-done.came_ref, bf16[2,128,512]{2,1,0:T(8,128)(2,1)S(1)} %bitcast.3, bf16[2,128,512]{2,1,0:T(8,128)(2,1)S(1)} %collective-permute-done.3.other_ref), custom_call_target="tpu_custom_call" | custom-call | flops 805306368 | bytes 4456448 | tf_op jit(solution)/shard_map/pallas_call | solution.py:137
  64.2 0.0 copy-start
  64.3 15.4 %all_to_all.16.arrived_ref = bf16[4,384,256]{2,1,0:T(8,128)(2,1)S(1)} all-to-all(bf16[4,384,256]{2,1,0:T(8,128)(2,1)S(1)} %shard_map.38), channel_id=1, replica_groups=mesh['z_far'=4,'z_near'=4,'y_hi'=2,'core'=2,'x'=4,'y_lo'=2] {'x'}, dimensions={0} | all-to-all | bytes 1572864 | tf_op jit(solution)/shard_map/all_to_all | solution.py:33
  79.6 0.0 copy-done
  79.6 0.8 shard_map.39
  (4 shorter events, 0.1 us)
Async XLA Ops:
  4.0 20.9 %all-to-all-start = ((bf16[16,16,512]{2,1,0:T(8,128)(2,1)}), bf16[16,16,512]{2,1,0:T(8,128)(2,1)S(1)}, u32[]{:S(2)}, u32[]{:S(2)}) async-start(bf16[16,16,512]{2,1,0:T(8,128)(2,1)} %bitcast), calls=%async_computation | async-start | bytes 524288 | tf_op jit(solution)/shard_map/all_to_all | solution.py:33
  14.3 47.8 %collective-permute-start = (bf16[1536,512]{1,0:T(8,128)(2,1)}, bf16[1536,512]{1,0:T(8,128)(2,1)S(1)}, u32[]{:S(2)}, u32[]{:S(2)}) collective-permute-start(bf16[1536,512]{1,0:T(8,128)(2,1)} %get-tuple-element.9), channel_id=1, source_target_pairs={{0,1},{1,0},{2,3},{3,2},{4,5},{5,4},{6,7},{7,6},{8,9},{9,8},{10,11... | collective-permute-start | bytes 4718600 | tf_op jit(solution)/shard_map/ppermute | solution.py:174
  25.0 10.1 %collective-permute-start.1 = (f32[16,512]{1,0:T(8,128)S(1)}, f32[16,512]{1,0:T(8,128)S(1)}, u32[]{:S(2)}, u32[]{:S(2)}) collective-permute-start(f32[16,512]{1,0:T(8,128)S(1)} %convert_reduce_fusion), channel_id=1, source_target_pairs={{128,256},{256,128},{384,0},{0,384},{8,136},{136,8},{264,392},{392... | collective-permute-start | bytes 98312 | tf_op jit(solution)/shard_map/ppermute | solution.py:178
  35.1 9.3 %collective-permute-start.2 = (f32[16,512]{1,0:T(8,128)S(1)}, f32[16,512]{1,0:T(8,128)S(1)}, u32[]{:S(2)}, u32[]{:S(2)}) collective-permute-start(f32[16,512]{1,0:T(8,128)S(1)} %add.6), channel_id=1, source_target_pairs={{0,128},{128,0},{256,384},{384,256},{136,264},{264,136},{392,8},{8... | collective-permute-start | bytes 98312 | tf_op jit(solution)/shard_map/ppermute | solution.py:178
  58.2 5.0 %collective-permute-start.3 = (bf16[2,128,512]{2,1,0:T(8,128)(2,1)S(1)}, bf16[2,128,512]{2,1,0:T(8,128)(2,1)S(1)}, u32[]{:S(2)}, u32[]{:S(2)}) collective-permute-start(bf16[2,128,512]{2,1,0:T(8,128)(2,1)S(1)} %bitcast.2), channel_id=1, source_target_pairs={{0,8},{8,0},{1,9},{9,1},{2,10},{10,2},{3,11},{11,3},{4,12},{12,4},... | collective-permute-start | bytes 786440 | tf_op jit(solution)/shard_map/ppermute | solution.py:182
  64.2 15.4 %copy-start = (bf16[384,256]{1,0:T(8,128)(2,1)S(1)}, bf16[384,256]{1,0:T(8,128)(2,1)}, u32[]{:S(2)}) copy-start(bf16[384,256]{1,0:T(8,128)(2,1)} %prior_ref.1) | copy-start | bytes 589828
